TPU v7x, 32 devices: a whole 2x2x4 slice. The times are simulated.
32 devices in a mesh: seq: 8 (over z, y), dp: 4 (over x, core).
Axes of the slice: x: 2, y: 2, z: 4, core: 2. Of those that a mesh axis runs over, the one named last changes fastest.
Arguments:
- queries: bfloat16 [4, 1024, 1024], P('dp', 'seq'), may hold values from -150 to 150
- key_states: bfloat16 [4, 1024, 1024], P('dp', 'seq'), may hold values from -6 to 6
- values: bfloat16 [4, 1024, 1024], P('dp', 'seq'), may hold values from -6 to 6
- w_out: bfloat16 [1024, 1024], replicated, may hold values from -0.1875 to 0.1875
- cotangent: bfloat16 [4, 1024, 1024], P('dp', 'seq'), may hold values from -6 to 6
- neighbours: int32 [4, 8, 2], P('dp', 'seq'), may hold values from 0 to 7, as said below
- counts: int32 [4, 8], P('dp', 'seq'), may hold values from 1 to 2
Outputs:
- output: bfloat16 [4, 1024, 1024], P('dp', 'seq')
- grad_queries: bfloat16 [4, 1024, 1024], P('dp', 'seq')
- grad_keys: bfloat16 [4, 1024, 1024], P('dp', 'seq')
- grad_values: bfloat16 [4, 1024, 1024], P('dp', 'seq')
- grad_w_out: float32 [1024, 1024], P(('seq', 'dp'))
Inputs may be any that keep to these rules, and one draw needn't show every extreme that they name: `neighbours`: entries j < counts[s, p] of patch p's list are distinct patches other than p, at most 1 patches away from p; the later entries equal p.
All inputs are finite; a program needn't handle non-finite values.
Results may differ from a plain program's by a relative error of at most 0.029.
Values may be sent and summed in bfloat16 or wider, within the bound.
No kernel may reach another device: no remote copies, remote signals or barrier semaphores. Data moves between devices by JAX's collectives and lax.ppermute only.
A program may use at most 64 MiB of HBM per device.

v0:
```python
import functools
import math

import jax
import jax.numpy as jnp
from jax import lax
from jax.experimental import pallas as pl
from jax.experimental.pallas import tpu as pltpu
from jax.sharding import PartitionSpec as P

HD = 128
VMEM_LIMIT = 12 * 1024 * 1024
F32 = jnp.float32
BF16 = jnp.bfloat16
VMEM = pl.BlockSpec(memory_space=pltpu.VMEM)
SMEM = pl.BlockSpec(memory_space=pltpu.SMEM)
HBM = pl.BlockSpec(memory_space=pltpu.HBM)
ANY = pl.BlockSpec(memory_space=pl.ANY)
FLAG_ROWS = 16


def dot(a, b, ca, cb):
    return lax.dot_general(a, b, (((ca,), (cb,)), ((), ())), preferred_element_type=F32)


def bit_reversed(index, bits):
    out = 0
    for b in range(bits):
        out = out * 2 + ((index >> b) & 1)
    return out


def shape_of(*dims, dtype=BF16):
    return jax.ShapeDtypeStruct(dims, dtype)


def call(body, out_shape, in_specs, name, scratch=()):
    return pl.pallas_call(
        body,
        out_shape=out_shape,
        in_specs=in_specs,
        out_specs=(VMEM,) * len(out_shape),
        scratch_shapes=list(scratch),
        compiler_params=pltpu.CompilerParams(vmem_limit_bytes=VMEM_LIMIT),
        cost_estimate=pl.CostEstimate(flops=0, bytes_accessed=0, transcendentals=0),
        name=name,
    )


def head_cols(pair, parity):
    return pl.ds(pl.multiple_of((2 * pair + parity) * HD, HD), HD)


def listed_flags(me, listed, live):
    far_patch = jnp.where(me % 2 == 0, me - 1, me + 1)
    near, far = jnp.int32(0), jnp.int32(0)
    for slot in range(listed.shape[1]):
        used = slot < live[0, 0]
        near = jnp.where(used & (listed[0, slot] == (me ^ 1)), 1, near)
        far = jnp.where(used & (listed[0, slot] == far_patch), 1, far)
    return near, far


def pack_kv_kernel(who, k, v, kv_send, kv_keep, sems):
    mine = who[0] & 1
    tokens, half = kv_send.shape[0] // 2, kv_send.shape[1]
    copies = []
    for target, parity in ((kv_send, 1 - mine), (kv_keep, mine)):
        for source, row in ((k, 0), (v, tokens)):
            for j in range(half // HD):
                item = pltpu.make_async_copy(
                    source.at[:, head_cols(j, parity)],
                    target.at[row : row + tokens, j * HD : (j + 1) * HD],
                    sems.at[len(copies)],
                )
                item.start()
                copies.append(item)
    for item in copies:
        item.wait()


def in_hbm(x):
    return pltpu.with_memory_space_constraint(x, pltpu.HBM)


def pack_kv(who, k, v):
    tokens, features = k.shape
    kv = shape_of(2 * tokens, features // 2)
    return call(
        pack_kv_kernel,
        (kv, kv),
        [SMEM, HBM, HBM],
        "pack_keys_values",
        scratch=[pltpu.SemaphoreType.DMA((2 * features // HD,))],
    )(who, in_hbm(k), in_hbm(v))


def pack_q_kernel(who, listed, live, q, q_send, q_keep):
    mine = who[0] & 1
    tokens, half = q_keep.shape
    for j in range(half // HD):
        cols = slice(j * HD, (j + 1) * HD)
        q_keep[:, cols] = q[:, head_cols(j, mine)]
        q_send[:tokens, cols] = q[:, head_cols(j, 1 - mine)]
    near, far = listed_flags(who[0], listed, live)
    left = lax.broadcasted_iota(jnp.int32, (FLAG_ROWS, half), 1) < half // 2
    q_send[tokens : tokens + FLAG_ROWS, :] = jnp.where(left, near, far).astype(F32).astype(BF16)


def pack_q(who, listed, live, q):
    tokens, features = q.shape
    return call(
        pack_q_kernel,
        (shape_of(tokens + FLAG_ROWS, features // 2), shape_of(tokens, features // 2)),
        [SMEM] * 3 + [VMEM],
        "pack_queries",
    )(who, listed, live, q)


def far_slot(me):
    return 1 - ((me & 1) ^ ((me >> 1) & 1))


def forward_kernel(
    direct, n_dp, who, listed, live, q_own, q_par, own, par, far_own, far_par, after,
    probs, att_own, att_back, att_t,
):
    rate = math.log2(math.e) / math.sqrt(HD)
    tokens, half = q_own.shape
    pairs = half // HD
    me = who[0]
    near_flag, far_flag = listed_flags(me, listed, live)
    barred = lambda x: jnp.where(x > 0, 0.0, -jnp.inf)
    theirs = q_par[tokens : tokens + FLAG_ROWS, :].astype(F32)[:1]
    left = lax.broadcasted_iota(jnp.int32, (1, 2 * tokens), 1) < tokens
    near_par = barred(jnp.broadcast_to(theirs[:, :1], (1, 2 * tokens)))
    far_par_bias = barred(jnp.broadcast_to(theirs[:, half - 1 :], (1, 2 * tokens)))
    bias = (
        jnp.where(left, 0.0, near_par),
        jnp.where(left, barred(near_flag), 0.0),
        jnp.where(left, barred(far_flag), far_par_bias),
    )
    for j in range(pairs):
        cols = slice(j * HD, (j + 1) * HD)
        qo, qp = q_own[:, cols], q_par[:tokens, cols]
        q = jnp.concatenate([qo, qp], axis=0)
        k = jnp.concatenate([own[:tokens, cols], par[:tokens, cols]], axis=0)
        v = jnp.concatenate([own[tokens:, cols], par[tokens:, cols]], axis=0)
        near = dot(k, q, 1, 1)
        far = jnp.concatenate(
            [dot(far_own[:tokens, cols], qo, 1, 1), dot(far_par[:tokens, cols], qp, 1, 1)], axis=1
        )
        s = [near[:tokens] + bias[0], near[tokens:] + bias[1], far + bias[2]]
        top = jnp.max(jnp.maximum(jnp.maximum(s[0], s[1]), s[2]), axis=0, keepdims=True)
        e = [jnp.exp2((x - top) * rate) for x in s]
        inv = 1.0 / jnp.sum(e[0] + e[1] + e[2], axis=0, keepdims=True)
        low = [(x * inv).astype(BF16) for x in e]
        for i in range(3):
            probs[j, i * tokens : (i + 1) * tokens, :] = low[i]
        vfo, vfp = far_own[tokens:, cols], far_par[tokens:, cols]
        o_t = dot(v, jnp.concatenate(low[:2], axis=0), 0, 0)
        o_t += jnp.concatenate(
            [dot(vfo, low[2][:, :tokens], 0, 0), dot(vfp, low[2][:, tokens:], 0, 0)], axis=1
        )
        o = o_t.T.astype(BF16)
        att_own[:, cols] = o[:tokens]
        att_back[:, cols] = o[tokens:]
        o_low = o_t.astype(BF16)
        if direct:
            rows = HD // n_dp
            place = bit_reversed(j ^ (me >> 1), (pairs - 1).bit_length())
            for d in range(n_dp):
                block = bit_reversed((d ^ who[1]) >> 1, (n_dp // 2 - 1).bit_length())
                start = pl.multiple_of((block * pairs + place) * rows, rows)
                att_t[(d ^ who[1]) & 1, pl.ds(start, rows), :] = o_low[d * rows : (d + 1) * rows, :]
        else:
            att_t[cols, :] = o_low


def forward(who, listed, live, inputs, after, n_seq, n_dp):
    tokens, half = inputs[0].shape
    features = 2 * half
    heads, pairs = features // HD, half // HD
    direct = n_seq == heads and HD % n_dp == 0 and (HD // n_dp) % 16 == 0
    one = shape_of(tokens, half)
    turned = shape_of(2, half // 2, 2 * tokens) if direct else shape_of(half, 2 * tokens)
    probs, att_own, att_back, turned = call(
        functools.partial(forward_kernel, direct, n_dp),
        (shape_of(pairs, 3 * tokens, 2 * tokens), one, one, turned),
        [SMEM] * 3 + [VMEM] * 6 + [ANY],
        "patch_forward",
    )(who, listed, live, *inputs, after)
    if not direct:
        here = who[0]
        bits, d_bits = (n_seq - 1).bit_length(), (n_dp // 2 - 1).bit_length()
        order = jnp.array([bit_reversed(i, bits) for i in range(n_seq)], jnp.int32) ^ here
        d_order = [bit_reversed(i, d_bits) * 2 + c for c in range(2) for i in range(n_dp // 2)]
        full = jnp.zeros((heads // 2, 2, HD, 2 * tokens), BF16)
        full = lax.dynamic_update_slice(
            full, turned.reshape(heads // 2, 1, HD, 2 * tokens), (0, here & 1, 0, 0)
        )
        full = full.reshape(n_seq, n_dp, features // (n_seq * n_dp), 2 * tokens)
        full = jnp.take(full, order, axis=0)
        full = jnp.take(full, jnp.array(d_order, jnp.int32) ^ who[1], axis=1).transpose(1, 0, 2, 3)
        turned = full.reshape(2, features // 2, 2 * tokens)
    return probs, att_own, att_back, turned, 2 if direct else 1


def backward_kernel(
    who, q_own, q_par, own, par, far_own, far_par, ga_full, cot_par, w, probs,
    grads, ga, edge_a, edge_b,
):
    scale = 1.0 / math.sqrt(HD)
    tokens, half = q_own.shape
    slot = far_slot(who[0])
    last = slice(2 * tokens, 3 * tokens)
    for j in range(half // HD):
        cols = slice(j * HD, (j + 1) * HD)
        mine = head_cols(j, who[0] & 1)
        go = ga_full[:, mine]
        gp = dot(cot_par[...], w[mine, :], 1, 1).astype(BF16)
        g_both = jnp.concatenate([go, gp], axis=0)
        ga[:, cols] = g_both
        qo, qp = q_own[:, cols], q_par[:tokens, cols]
        v = jnp.concatenate([own[tokens:, cols], par[tokens:, cols]], axis=0)
        vfo, vfp = far_own[tokens:, cols], far_par[tokens:, cols]
        gn = dot(v, g_both, 1, 1)
        g = [
            gn[:tokens],
            gn[tokens:],
            jnp.concatenate([dot(vfo, go, 1, 1), dot(vfp, gp, 1, 1)], axis=1),
        ]
        p = [probs[j, i * tokens : (i + 1) * tokens, :].astype(F32) for i in range(3)]
        delta = jnp.sum(p[0] * g[0] + p[1] * g[1] + p[2] * g[2], axis=0, keepdims=True)
        ds = [(p[i] * (g[i] - delta)).astype(BF16) for i in range(3)]
        for i in range(3):
            grads[j, i * tokens : (i + 1) * tokens, :] = ds[i]
        dfo, dfp = ds[2][:, :tokens], ds[2][:, tokens:]
        own_far = jnp.concatenate(
            [dot(dfo, qo, 1, 0) * scale, dot(probs[j, last, :tokens], go, 1, 0)], axis=0
        ).astype(BF16)
        par_far = jnp.concatenate(
            [dot(dfp, qp, 1, 0) * scale, dot(probs[j, last, tokens:], gp, 1, 0)], axis=0
        ).astype(BF16)
        edge_a[:, cols] = jnp.where(slot == 0, own_far, par_far)
        edge_b[:, cols] = jnp.where(slot == 0, par_far, own_far)


def backward(who, inputs, ga_full, cot_par, w, probs):
    tokens, half = inputs[0].shape
    return call(
        backward_kernel,
        (shape_of(*probs.shape),) + (shape_of(2 * tokens, half),) * 3,
        [SMEM] + [VMEM] * 10,
        "patch_backward",
    )(who, *inputs, ga_full, cot_par, w, probs)


def gradient_kernel(
    q_own, q_par, own, par, far_own, far_par, ga, probs, grads, dq_own, dq_back, d_own, d_par
):
    scale = 1.0 / math.sqrt(HD)
    tokens, half = q_own.shape
    near, last = slice(0, 2 * tokens), slice(2 * tokens, 3 * tokens)
    for j in range(half // HD):
        cols = slice(j * HD, (j + 1) * HD)
        q = jnp.concatenate([q_own[:, cols], q_par[:tokens, cols]], axis=0)
        k = jnp.concatenate([own[:tokens, cols], par[:tokens, cols]], axis=0)
        kfo, kfp = far_own[:tokens, cols], far_par[:tokens, cols]
        low, dsn = probs[j, near, :], grads[j, near, :]
        dfo, dfp = grads[j, last, :tokens], grads[j, last, tokens:]
        dq = dot(dsn, k, 0, 0) + jnp.concatenate([dot(dfo, kfo, 0, 0), dot(dfp, kfp, 0, 0)], axis=0)
        dq = (dq * scale).astype(BF16)
        dq_own[:, cols] = dq[:tokens]
        dq_back[:, cols] = dq[tokens:]
        dk = (dot(dsn, q, 1, 0) * scale).astype(BF16)
        dv = dot(low, ga[:, cols], 1, 0).astype(BF16)
        d_own[:tokens, cols] = dk[:tokens]
        d_par[:tokens, cols] = dk[tokens:]
        d_own[tokens:, cols] = dv[:tokens]
        d_par[tokens:, cols] = dv[tokens:]


def gradients(inputs, ga, probs, grads):
    tokens, half = inputs[0].shape
    one, kv = shape_of(tokens, half), shape_of(2 * tokens, half)
    return call(
        gradient_kernel, (one, one, kv, kv), [VMEM] * 9, "patch_gradients"
    )(*inputs, ga, probs, grads)


def weight_kernel(att_keep, att_core, own, par, core_own, core_par, keep, send):
    size = keep.shape[0]
    tokens = own.shape[0]
    for target, start in ((send, size), (keep, 0)):
        rows = slice(start, start + size)
        total = dot(att_keep[rows, :tokens], own[...], 1, 0)
        total += dot(att_keep[rows, tokens:], par[...], 1, 0)
        total += dot(att_core[rows, :tokens], core_own[...], 1, 0)
        total += dot(att_core[rows, tokens:], core_par[...], 1, 0)
        target[...] = total.astype(target.dtype)


def weight_terms(*operands):
    rows = operands[0].shape[0]
    tokens, width = operands[2].shape
    return call(
        weight_kernel,
        (shape_of(rows // 2, width, dtype=F32), shape_of(rows // 2, width)),
        [VMEM] * 6,
        "weight_terms",
    )(*operands)


def output_kernel(who, att_own, att_back, w, out, att):
    mine = who[0] & 1
    for j in range(att_own.shape[1] // HD):
        cols = slice(j * HD, (j + 1) * HD)
        att[:, head_cols(j, mine)] = att_own[:, cols]
        att[:, head_cols(j, 1 - mine)] = att_back[:, cols]
    out[...] = dot(att[...], w[...], 1, 0).astype(BF16)


def finish_output(who, att_own, att_back, w):
    tokens = att_own.shape[0]
    return call(
        output_kernel,
        (shape_of(tokens, w.shape[1]),),
        [SMEM] + [VMEM] * 3,
        "finish_output",
        scratch=[pltpu.VMEM((tokens, w.shape[0]), BF16)],
    )(who, att_own, att_back, w)[0]


def final_kernel(who, dq_own, dq_back, own, far_a, far_b, home, dq, dk, dv):
    mine = who[0] & 1
    slot = far_slot(who[0])
    tokens = dk.shape[0]
    for j in range(own.shape[1] // HD):
        cols = slice(j * HD, (j + 1) * HD)
        dq[:, head_cols(j, mine)] = dq_own[:, cols]
        dq[:, head_cols(j, 1 - mine)] = dq_back[:, cols]
        for i, target in ((0, dk), (1, dv)):
            rows = slice(i * tokens, (i + 1) * tokens)
            far = jnp.where(slot == 0, far_a[rows, cols].astype(F32), far_b[rows, cols].astype(F32))
            target[:, head_cols(j, mine)] = (own[rows, cols].astype(F32) + far).astype(BF16)
            target[:, head_cols(j, 1 - mine)] = home[rows, cols]


def finish_gradients(who, dq_own, dq_back, own, far, home):
    tokens, half = dq_own.shape
    return call(
        final_kernel,
        (shape_of(tokens, 2 * half),) * 3,
        [SMEM] + [VMEM] * 6,
        "finish_gradients",
    )(who, dq_own, dq_back, own, *far, home)


def on_device(queries, key_states, values, w_out, cotangent, neighbours, counts):
    n_seq, n_dp = lax.axis_size("seq"), lax.axis_size("dp")
    me, my_dp = lax.axis_index("seq").astype(jnp.int32), lax.axis_index("dp").astype(jnp.int32)
    who = jnp.stack([me, my_dp])
    cot = cotangent[0]

    swap = [(i, i ^ 1) for i in range(n_seq)]
    relay = [(i, i + 2) for i in range(0, n_seq, 2) if i + 2 < n_seq]
    relay += [(i, i - 2) for i in range(1, n_seq, 2) if i - 2 >= 0]
    outer = [(b, a) for a, b in relay]
    edges = [[], []]
    for i in range(n_seq):
        edges[0].append((i, i ^ 2))
        other = i + 2 if (i >> 1) & 1 else i - 2
        if 0 <= other < n_seq:
            edges[1].append((i, other))
    send = lambda x, pairs: lax.ppermute(x, "seq", pairs)
    across = lambda x, k: lax.ppermute(x, "dp", [(i, i ^ k) for i in range(n_dp)])

    kv_send, own = pack_kv(who, key_states[0], values[0])
    q_send, q_own = pack_q(who, neighbours[0], counts, queries[0])
    par = send(kv_send, swap)
    far_par = send(own, outer)
    core_own = across(cot, 1)
    ga_full = dot(cot, w_out, 1, 1).astype(BF16)
    cot_par = send(cot, swap)
    q_par = send(q_send, swap)
    far_own = send(par, relay)
    core_par = across(cot_par, 1)

    inputs = (q_own, q_par, own, par, far_own, far_par)
    probs, att_own, att_back, att_t, step = forward(
        who, neighbours[0], counts, inputs, ga_full, n_seq, n_dp
    )
    att_core = across(att_t[1], 1)
    att_back = send(att_back, swap)
    grads, ga, *leaving = backward(who, inputs, ga_full, cot_par, w_out, probs)
    far = [send(leaving[i], edges[i]) for i in range(2)]
    keep, out = weight_terms(att_t[0], att_core, cot, cot_par, core_own, core_par)
    dq_own, dq_back, d_own, d_par = gradients(inputs, ga, probs, grads)
    dq_back = send(dq_back, swap)
    returned = jnp.where(far_slot(me) == 0, far[1], far[0])
    home = send((d_par.astype(F32) + returned.astype(F32)).astype(BF16), swap)

    hops = []
    bit = 2
    while bit < n_dp:
        hops.append(("dp", n_dp, bit))
        bit *= 2
    while step < n_seq:
        hops.append(("seq", n_seq, step))
        step *= 2
    for place, (axis, count, bit) in enumerate(hops):
        total = keep + lax.ppermute(out, axis, [(i, i ^ bit) for i in range(count)]).astype(F32)
        rows = total.shape[0] // 2
        if place + 1 < len(hops):
            keep, out = total[:rows], total[rows:].astype(BF16)

    output = finish_output(who, att_own, att_back, w_out)
    dq, dk, dv = finish_gradients(who, dq_own, dq_back, d_own, far, home)
    return (output[None], dq[None], dk[None], dv[None], total)


def solution(mesh):
    placed = (
        P("dp", "seq", None),
        P("dp", "seq", None),
        P("dp", "seq", None),
        P(),
        P("dp", "seq", None),
        P("dp", "seq", None),
        P("dp", "seq"),
    )
    return jax.shard_map(
        on_device,
        mesh=mesh,
        in_specs=placed,
        out_specs=(
            P("dp", "seq", None),
            P("dp", "seq", None),
            P("dp", "seq", None),
            P("dp", "seq", None),
            P(("seq", "dp"), None),
        ),
        check_vma=False,
    )
```

profile of v0, /device:TPU:0, one launch (start us, length us, event | category | flops | bytes accessed | tf_op | source)
XLA Modules:
  0.0 61.2 jit_solution(16857550437237719896)
XLA Ops:
  0.6 0.0 copy-start.20
  0.6 0.1 pad_add_fusion.who
  0.7 1.7 %pack_keys_values.1 = (bf16[256,512]{1,0:T(8,128)(2,1)S(1)}, bf16[256,512]{1,0:T(8,128)(2,1)S(1)}) custom-call(s32[2]{0:T(128)S(1)} %pad_add_fusion.who, bf16[128,1024]{1,0:T(8,128)(2,1)} %bitcast.24, bf16[128,1024]{1,0:T(8,128)(2,1)} %bitcast.25), custom_call_target="tpu_custom_call" | custom-call | tf_op jit(solution)/shard_map/pack_keys_values/pallas_call | solution.py:89
  2.4 3.0 %collective-permute-start.1 = (bf16[256,512]{1,0:T(8,128)(2,1)S(1)}, bf16[256,512]{1,0:T(8,128)(2,1)S(1)}, u32[]{:S(2)}, u32[]{:S(2)}) collective-permute-start(bf16[256,512]{1,0:T(8,128)(2,1)S(1)} %get-tuple-element.29), channel_id=1, source_target_pairs={{0,4},{4,0},{8,12},{12,8},{16,20},{20,16},{24,28},{28,24},{1,5},{5... | collective-permute-start | bytes 786440 | tf_op jit(solution)/shard_map/ppermute | solution.py:376
  5.5 0.0 collective-permute-start.11
  5.5 0.2 collective-permute-start.5
  6.3 0.0 copy-start.14
  6.3 0.9 %copy-done.14 = bf16[1,128,1024]{2,1,0:T(8,128)(2,1)S(1)} copy-done((bf16[1,128,1024]{2,1,0:T(8,128)(2,1)S(1)}, bf16[1,128,1024]{2,1,0:T(8,128)(2,1)}, u32[]{:S(2)}) %copy-start.14) | copy-done | bytes 262168
  7.2 0.7 %copy-done.19 = s32[1,1,2]{2,1,0:T(1,128)S(1)} copy-done((s32[1,1,2]{2,1,0:T(1,128)S(1)}, s32[1,1,2]{2,1,0:T(1,128)}, u32[]{:S(2)}) %copy-start.19) | copy-done | bytes 32
  7.9 0.6 %pack_queries.1 = (bf16[144,512]{1,0:T(8,128)(2,1)S(1)}, bf16[128,512]{1,0:T(8,128)(2,1)S(1)}) custom-call(s32[2]{0:T(128)S(1)} %pad_add_fusion.who, s32[1,2]{1,0:T(1,128)S(1)} %bitcast.22, s32[1,1]{1,0:T(1,128)S(6)} %copy.12.live, bf16[128,1024]{1,0:T(8,128)(2,1)S(1)} %bitcast.21), custom_call_target="tpu_custom_call" | custom-call | tf_op jit(solution)/shard_map/pack_queries/pallas_call | solution.py:112
  8.5 0.0 copy-start.5
  8.5 1.9 %collective-permute-start = (bf16[144,512]{1,0:T(8,128)(2,1)S(1)}, bf16[144,512]{1,0:T(8,128)(2,1)S(1)}, u32[]{:S(2)}, u32[]{:S(2)}) collective-permute-start(bf16[144,512]{1,0:T(8,128)(2,1)S(1)} %get-tuple-element.27), channel_id=1, source_target_pairs={{0,4},{4,0},{8,12},{12,8},{16,20},{20,16},{24,28},{28,24},{1,5},{5... | collective-permute-start | bytes 442376 | tf_op jit(solution)/shard_map/ppermute | solution.py:376
  10.5 1.4 %collective-permute-start.3 = (bf16[256,512]{1,0:T(8,128)(2,1)S(1)}, bf16[256,512]{1,0:T(8,128)(2,1)S(1)}, u32[]{:S(2)}, u32[]{:S(2)}) collective-permute-start(bf16[256,512]{1,0:T(8,128)(2,1)S(1)} %get-tuple-element.28.own), channel_id=1, source_target_pairs={{8,0},{16,8},{24,16},{4,12},{12,20},{20,28},{9,1},{17,9},{25,17},{... | collective-permute-start | bytes 786440 | tf_op jit(solution)/shard_map/ppermute | solution.py:376
  11.9 0.7 %collective-permute-done.1.par = bf16[256,512]{1,0:T(8,128)(2,1)S(1)} collective-permute-done((bf16[256,512]{1,0:T(8,128)(2,1)S(1)}, bf16[256,512]{1,0:T(8,128)(2,1)S(1)}, u32[]{:S(2)}, u32[]{:S(2)}) %collective-permute-start.1) | collective-permute-done | bytes 262176 | tf_op jit(solution)/shard_map/ppermute | solution.py:376
  12.6 4.0 %collective-permute-start.2 = (bf16[256,512]{1,0:T(8,128)(2,1)S(1)}, bf16[256,512]{1,0:T(8,128)(2,1)S(1)}, u32[]{:S(2)}, u32[]{:S(2)}) collective-permute-start(bf16[256,512]{1,0:T(8,128)(2,1)S(1)} %collective-permute-done.1.par), channel_id=1, source_target_pairs={{0,8},{8,16},{16,24},{12,4},{20,12},{28,20},{1,9},{9,17},{17,25},{... | collective-permute-start | bytes 786440 | tf_op jit(solution)/shard_map/ppermute | solution.py:376
  16.6 2.5 %convolution_convert_fusion.after.ga_full = bf16[128,1024]{1,0:T(8,128)(2,1)S(1)} fusion(bf16[1024,1024]{1,0:T(8,128)(2,1)} %w.3, bf16[1,128,1024]{2,1,0:T(8,128)(2,1)} %param.11), kind=kOutput, calls=%fused_computation | convolution fusion | flops 268566528 | bytes 2621440 | tf_op jit(solution)/shard_map/dot_general | solution.py:23
  19.2 0.0 copy-start
  19.2 0.0 collective-permute-done.5.cot_par.par
  19.2 0.1 collective-permute-start.12
  19.3 1.3 %collective-permute-done.q_par = bf16[144,512]{1,0:T(8,128)(2,1)S(1)} collective-permute-done((bf16[144,512]{1,0:T(8,128)(2,1)S(1)}, bf16[144,512]{1,0:T(8,128)(2,1)S(1)}, u32[]{:S(2)}, u32[]{:S(2)}) %collective-permute-start) | collective-permute-done | bytes 147488 | tf_op jit(solution)/shard_map/ppermute | solution.py:376
  20.5 0.1 collective-permute-done.3.far_par
  20.6 1.2 %collective-permute-done.2.far_own = bf16[256,512]{1,0:T(8,128)(2,1)S(1)} collective-permute-done((bf16[256,512]{1,0:T(8,128)(2,1)S(1)}, bf16[256,512]{1,0:T(8,128)(2,1)S(1)}, u32[]{:S(2)}, u32[]{:S(2)}) %collective-permute-start.2) | collective-permute-done | bytes 262176 | tf_op jit(solution)/shard_map/ppermute | solution.py:376
  21.8 0.0 copy-done.20
  21.8 2.1 %patch_forward.1 = (bf16[4,384,256]{2,1,0:T(8,128)(2,1)S(1)}, bf16[128,512]{1,0:T(8,128)(2,1)S(1)}, bf16[128,512]{1,0:T(8,128)(2,1)S(1)}, bf16[2,256,256]{2,1,0:T(8,128)(2,1)S(1)}) custom-call(s32[2]{0:T(128)S(1)} %pad_add_fusion.who, s32[1,2]{1,0:T(1,128)S(1)} %bitcast.23, s32[1,1]{1,0:T(1,128)S(6)} %copy.12.live, ...), custom_call_target="tpu_custom_call" | custom-call | tf_op jit(solution)/shard_map/patch_forward/pallas_call | solution.py:187
  24.0 0.0 copy-start.21
  24.0 0.6 %copy-done.21 = bf16[128,512]{1,0:T(8,128)(2,1)} copy-done((bf16[128,512]{1,0:T(8,128)(2,1)}, bf16[128,512]{1,0:T(8,128)(2,1)S(1)}, u32[]{:S(2)}) %copy-start.21) | copy-done | bytes 131096
  24.6 0.1 collective-permute-start.10
  24.7 0.0 collective-permute-done.11.core_own
  24.7 0.0 collective-permute-done.12.core_par
  24.7 1.3 %collective-permute-done.10.att_core = bf16[256,256]{1,0:T(8,128)(2,1)S(1)} collective-permute-done((bf16[256,256]{1,0:T(8,128)(2,1)S(1)}, bf16[256,256]{1,0:T(8,128)(2,1)S(1)}, u32[]{:S(2)}, u32[]{:S(2)}) %collective-permute-start.10) | collective-permute-done | bytes 131104 | tf_op jit(solution)/shard_map/ppermute | solution.py:377
  26.1 0.0 copy-done.7
  26.1 1.2 %weight_terms.1 = (f32[128,1024]{1,0:T(8,128)S(1)}, bf16[128,1024]{1,0:T(8,128)(2,1)}) custom-call(bf16[256,256]{1,0:T(8,128)(2,1)S(1)} %get-tuple-element.48.att_keep, bf16[256,256]{1,0:T(8,128)(2,1)S(1)} %collective-permute-done.10.att_core, bf16[128,1024]{1,0:T(8,128)(2,1)S(1)} %bitcast.20, bf16[128,1024]{1,0:T(8,128)(2,1)S(1)} %collective-permute-done.5.cot_par.par, ...), custom_call_target="tpu_custom_call" | custom-call | tf_op jit(solution)/shard_map/weight_terms/pallas_call | solution.py:307
  27.3 1.5 %collective-permute-start.13 = (bf16[128,1024]{1,0:T(8,128)(2,1)}, bf16[128,1024]{1,0:T(8,128)(2,1)}, u32[]{:S(2)}, u32[]{:S(2)}) collective-permute-start(bf16[128,1024]{1,0:T(8,128)(2,1)} %get-tuple-element.46), channel_id=1, source_target_pairs={{0,2},{1,3},{2,0},{3,1},{4,6},{5,7},{6,4},{7,5},{8,10},{9,11},{10,... | collective-permute-start | bytes 786440 | tf_op jit(solution)/shard_map/ppermute | solution.py:413
  28.8 3.8 %patch_backward.1 = (bf16[4,384,256]{2,1,0:T(8,128)(2,1)S(1)}, bf16[256,512]{1,0:T(8,128)(2,1)S(1)}, bf16[256,512]{1,0:T(8,128)(2,1)}, bf16[256,512]{1,0:T(8,128)(2,1)}) custom-call(s32[2]{0:T(128)S(1)} %pad_add_fusion.who, bf16[128,512]{1,0:T(8,128)(2,1)S(1)} %get-tuple-element.26.q_own, bf16[144,512]{1,0:T(8,128)(2,1)S(1)} %collective-permute-done.q_par, ...), custom_call_target="tpu_custom_call" | custom-call | tf_op jit(solution)/shard_map/patch_backward/pallas_call | solution.py:251
  32.5 0.0 copy-done.3
  32.6 0.9 %copy-done.8 = bf16[4,384,256]{2,1,0:T(8,128)(2,1)} copy-done((bf16[4,384,256]{2,1,0:T(8,128)(2,1)}, bf16[4,384,256]{2,1,0:T(8,128)(2,1)S(1)}, u32[]{:S(2)}) %copy-start.8) | copy-done | bytes 786456
  33.5 0.7 %copy-done.12 = bf16[256,512]{1,0:T(8,128)(2,1)} copy-done((bf16[256,512]{1,0:T(8,128)(2,1)}, bf16[256,512]{1,0:T(8,128)(2,1)S(1)}, u32[]{:S(2)}) %copy-start.12) | copy-done | bytes 262168
  34.2 2.5 %collective-permute-start.7 = (bf16[256,512]{1,0:T(8,128)(2,1)}, bf16[256,512]{1,0:T(8,128)(2,1)}, u32[]{:S(2)}, u32[]{:S(2)}) collective-permute-start(bf16[256,512]{1,0:T(8,128)(2,1)} %get-tuple-element.38), channel_id=1, source_target_pairs={{0,8},{4,12},{8,0},{12,4},{16,24},{20,28},{24,16},{28,20},{1,9},{5... | collective-permute-start | bytes 786440 | tf_op jit(solution)/shard_map/ppermute | solution.py:376
  36.7 1.4 %collective-permute-start.8 = (bf16[256,512]{1,0:T(8,128)(2,1)}, bf16[256,512]{1,0:T(8,128)(2,1)}, u32[]{:S(2)}, u32[]{:S(2)}) collective-permute-start(bf16[256,512]{1,0:T(8,128)(2,1)} %get-tuple-element.39), channel_id=1, source_target_pairs={{8,16},{12,20},{16,8},{20,12},{9,17},{13,21},{17,9},{21,13},{10,18... | collective-permute-start | bytes 786440 | tf_op jit(solution)/shard_map/ppermute | solution.py:376
  38.0 1.6 %collective-permute-start.4 = (bf16[128,512]{1,0:T(8,128)(2,1)}, bf16[128,512]{1,0:T(8,128)(2,1)S(1)}, u32[]{:S(2)}, u32[]{:S(2)}) collective-permute-start(bf16[128,512]{1,0:T(8,128)(2,1)} %copy-done.21), channel_id=1, source_target_pairs={{0,4},{4,0},{8,12},{12,8},{16,20},{20,16},{24,28},{28,24},{1,5},{5... | collective-permute-start | bytes 393224 | tf_op jit(solution)/shard_map/ppermute | solution.py:376
  39.6 0.9 %copy-done.2 = bf16[256,512]{1,0:T(8,128)(2,1)S(1)} copy-done((bf16[256,512]{1,0:T(8,128)(2,1)S(1)}, bf16[256,512]{1,0:T(8,128)(2,1)}, u32[]{:S(2)}) %copy-start.2) | copy-done | bytes 262168
  40.6 0.9 %copy-done.4 = bf16[256,512]{1,0:T(8,128)(2,1)S(1)} copy-done((bf16[256,512]{1,0:T(8,128)(2,1)S(1)}, bf16[256,512]{1,0:T(8,128)(2,1)}, u32[]{:S(2)}) %copy-start.4) | copy-done | bytes 262168
  41.5 0.9 %copy-done.6 = bf16[128,512]{1,0:T(8,128)(2,1)S(1)} copy-done((bf16[128,512]{1,0:T(8,128)(2,1)S(1)}, bf16[128,512]{1,0:T(8,128)(2,1)}, u32[]{:S(2)}) %copy-start.6) | copy-done | bytes 131096
  42.5 1.1 %copy-done.9 = bf16[4,384,256]{2,1,0:T(8,128)(2,1)S(1)} copy-done((bf16[4,384,256]{2,1,0:T(8,128)(2,1)S(1)}, bf16[4,384,256]{2,1,0:T(8,128)(2,1)}, u32[]{:S(2)}) %copy-start.9) | copy-done | bytes 786456
  43.6 0.9 %copy-done.13 = bf16[256,512]{1,0:T(8,128)(2,1)S(1)} copy-done((bf16[256,512]{1,0:T(8,128)(2,1)S(1)}, bf16[256,512]{1,0:T(8,128)(2,1)}, u32[]{:S(2)}) %copy-start.13) | copy-done | bytes 262168
  44.5 0.7 %patch_gradients.1 = (bf16[128,512]{1,0:T(8,128)(2,1)S(1)}, bf16[128,512]{1,0:T(8,128)(2,1)S(1)}, bf16[256,512]{1,0:T(8,128)(2,1)S(1)}, bf16[256,512]{1,0:T(8,128)(2,1)S(1)}) custom-call(bf16[128,512]{1,0:T(8,128)(2,1)S(1)} %copy-done.6, bf16[144,512]{1,0:T(8,128)(2,1)S(1)} %collective-permute-done.q_par, bf16[256,512]{1,0:T(8,128)(2,1)S(1)} %get-tuple-element.28.own, ...), custom_call_target="tpu_custom_call" | custom-call | tf_op jit(solution)/shard_map/patch_gradients/pallas_call | solution.py:287
  45.2 0.0 copy-start.16
  45.2 0.5 collective-permute-start.6
  45.7 0.0 collective-permute-done.13
  45.7 1.0 %convert_add_fusion = f32[128,1024]{1,0:T(8,128)S(1)} fusion(f32[128,1024]{1,0:T(8,128)S(1)} %copy-done.11, bf16[128,1024]{1,0:T(8,128)(2,1)} %collective-permute-done.13), kind=kLoop, calls=%fused_computation.1 | loop fusion | flops 262144 | bytes 1310720 | tf_op jit(solution)/shard_map/add | solution.py:413
  46.7 3.9 %collective-permute-start.14 = (bf16[64,1024]{1,0:T(8,128)(2,1)S(1)}, bf16[64,1024]{1,0:T(8,128)(2,1)S(1)}, u32[]{:S(2)}, u32[]{:S(2)}) collective-permute-start(bf16[64,1024]{1,0:T(8,128)(2,1)S(1)} %slice.36), channel_id=1, source_target_pairs={{0,8},{4,12},{8,0},{12,4},{16,24},{20,28},{24,16},{28,20},{1,9},{5... | collective-permute-start | bytes 393224 | tf_op jit(solution)/shard_map/ppermute | solution.py:413
  50.6 0.0 collective-permute-done.7.far_a
  50.6 0.0 collective-permute-done.8.far_b
  50.6 1.1 %add_convert_fusion = bf16[256,512]{1,0:T(8,128)(2,1)S(1)} fusion(bf16[256,512]{1,0:T(8,128)(2,1)S(1)} %get-tuple-element.40, bf16[256,512]{1,0:T(8,128)(2,1)} %collective-permute-done.8.far_b, bf16[256,512]{1,0:T(8,128)(2,1)} %collective-permute-done.7.far_a, pred[]{:T(512)S(6)} %eq.3), kind=kLoop, calls=%fused_computation.2 | loop fusion | flops 655360 | bytes 1048577 | tf_op jit(solution)/shard_map/convert_element_type | solution.py:402
  51.7 0.3 collective-permute-start.9
  52.0 1.5 %collective-permute-done.14 = bf16[64,1024]{1,0:T(8,128)(2,1)S(1)} collective-permute-done((bf16[64,1024]{1,0:T(8,128)(2,1)S(1)}, bf16[64,1024]{1,0:T(8,128)(2,1)S(1)}, u32[]{:S(2)}, u32[]{:S(2)}) %collective-permute-start.14) | collective-permute-done | bytes 131104 | tf_op jit(solution)/shard_map/ppermute | solution.py:413
  53.6 1.5 %collective-permute-start.15 = (bf16[32,1024]{1,0:T(8,128)(2,1)S(1)}, bf16[32,1024]{1,0:T(8,128)(2,1)S(1)}, u32[]{:S(2)}, u32[]{:S(2)}) collective-permute-start(bf16[32,1024]{1,0:T(8,128)(2,1)S(1)} %slice.37), channel_id=1, source_target_pairs={{0,16},{4,20},{8,24},{12,28},{16,0},{20,4},{24,8},{28,12},{1,17},{... | collective-permute-start | bytes 196616 | tf_op jit(solution)/shard_map/ppermute | solution.py:413
  55.1 0.0 collective-permute-done.4.att_back
  55.1 1.7 %finish_output.1 = bf16[128,1024]{1,0:T(8,128)(2,1)} custom-call(s32[2]{0:T(128)S(1)} %copy-done.18, bf16[128,512]{1,0:T(8,128)(2,1)S(1)} %copy-done.16, bf16[128,512]{1,0:T(8,128)(2,1)S(1)} %collective-permute-done.4.att_back, bf16[1024,1024]{1,0:T(8,128)(2,1)S(1)} %copy-done), custom_call_target="tpu_custom_call" | custom-call | tf_op jit(solution)/shard_map/finish_output/pallas_call | solution.py:326
  56.8 0.0 collective-permute-done.6.dq_back
  56.8 1.5 %collective-permute-done.9.home = bf16[256,512]{1,0:T(8,128)(2,1)S(1)} collective-permute-done((bf16[256,512]{1,0:T(8,128)(2,1)S(1)}, bf16[256,512]{1,0:T(8,128)(2,1)S(1)}, u32[]{:S(2)}, u32[]{:S(2)}) %collective-permute-start.9) | collective-permute-done | bytes 262176 | tf_op jit(solution)/shard_map/ppermute | solution.py:376
  58.4 2.1 %finish_gradients.1 = (bf16[128,1024]{1,0:T(8,128)(2,1)}, bf16[128,1024]{1,0:T(8,128)(2,1)}, bf16[128,1024]{1,0:T(8,128)(2,1)}) custom-call(s32[2]{0:T(128)S(1)} %copy-done.18, bf16[128,512]{1,0:T(8,128)(2,1)S(1)} %get-tuple-element.35.dq_own, bf16[128,512]{1,0:T(8,128)(2,1)S(1)} %collective-permute-done.6.dq_back, ...), custom_call_target="tpu_custom_call" | custom-call | tf_op jit(solution)/shard_map/finish_gradients/pallas_call | solution.py:352
  60.5 0.0 collective-permute-done.15
  60.5 0.7 %slice_add_fusion.1 = f32[32,1024]{1,0:T(8,128)} fusion(f32[64,1024]{1,0:T(8,128)S(1)} %slice_add_fusion, bf16[32,1024]{1,0:T(8,128)(2,1)S(1)} %collective-permute-done.15), kind=kLoop, calls=%fused_computation.6 | loop fusion | flops 65536 | bytes 327680 | tf_op jit(solution)/shard_map/add | solution.py:413
  (29 shorter events, 0.1 us)
Async XLA Ops:
  0.6 21.2 %copy-start.20 = (s32[1,1,2]{2,1,0:T(1,128)S(1)}, s32[1,1,2]{2,1,0:T(1,128)}, u32[]{:S(2)}) copy-start(s32[1,1,2]{2,1,0:T(1,128)} %param.12) | copy-start | bytes 28
  0.7 28.0 %copy-start.17 = (s32[2]{0:T(128)}, s32[2]{0:T(128)S(1)}, u32[]{:S(2)}) copy-start(s32[2]{0:T(128)S(1)} %pad_add_fusion.who) | copy-start | bytes 28
  2.4 10.2 %collective-permute-start.1 = (bf16[256,512]{1,0:T(8,128)(2,1)S(1)}, bf16[256,512]{1,0:T(8,128)(2,1)S(1)}, u32[]{:S(2)}, u32[]{:S(2)}) collective-permute-start(bf16[256,512]{1,0:T(8,128)(2,1)S(1)} %get-tuple-element.29), channel_id=1, source_target_pairs={{0,4},{4,0},{8,12},{12,8},{16,20},{20,16},{24,28},{28,24},{1,5},{5... | collective-permute-start | bytes 786440 | tf_op jit(solution)/shard_map/ppermute | solution.py:376
  5.5 19.3 %collective-permute-start.11 = (bf16[128,1024]{1,0:T(8,128)(2,1)}, bf16[128,1024]{1,0:T(8,128)(2,1)S(1)}, u32[]{:S(2)}, u32[]{:S(2)}) collective-permute-start(bf16[128,1024]{1,0:T(8,128)(2,1)} %bitcast.18), channel_id=1, source_target_pairs={{0,1},{1,0},{2,3},{3,2},{4,5},{5,4},{6,7},{7,6},{8,9},{9,8},{10,11... | collective-permute-start | bytes 786440 | tf_op jit(solution)/shard_map/ppermute | solution.py:377
  5.5 13.7 %collective-permute-start.5 = (bf16[128,1024]{1,0:T(8,128)(2,1)}, bf16[128,1024]{1,0:T(8,128)(2,1)S(1)}, u32[]{:S(2)}, u32[]{:S(2)}) collective-permute-start(bf16[128,1024]{1,0:T(8,128)(2,1)} %bitcast.19), channel_id=1, source_target_pairs={{0,4},{4,0},{8,12},{12,8},{16,20},{20,16},{24,28},{28,24},{1,5},{5... | collective-permute-start | bytes 786440 | tf_op jit(solution)/shard_map/ppermute | solution.py:376
  6.3 1.0 %copy-start.14 = (bf16[1,128,1024]{2,1,0:T(8,128)(2,1)S(1)}, bf16[1,128,1024]{2,1,0:T(8,128)(2,1)}, u32[]{:S(2)}) copy-start(bf16[1,128,1024]{2,1,0:T(8,128)(2,1)} %param.7) | copy-start | bytes 786436
  7.2 0.7 %copy-start.19 = (s32[1,1,2]{2,1,0:T(1,128)S(1)}, s32[1,1,2]{2,1,0:T(1,128)}, u32[]{:S(2)}) copy-start(s32[1,1,2]{2,1,0:T(1,128)} %param.12) | copy-start | bytes 28
  8.5 20.3 %copy-start.5 = (bf16[128,512]{1,0:T(8,128)(2,1)}, bf16[128,512]{1,0:T(8,128)(2,1)S(1)}, u32[]{:S(2)}) copy-start(bf16[128,512]{1,0:T(8,128)(2,1)S(1)} %get-tuple-element.26.q_own) | copy-start | bytes 393220
  8.5 12.0 %collective-permute-start = (bf16[144,512]{1,0:T(8,128)(2,1)S(1)}, bf16[144,512]{1,0:T(8,128)(2,1)S(1)}, u32[]{:S(2)}, u32[]{:S(2)}) collective-permute-start(bf16[144,512]{1,0:T(8,128)(2,1)S(1)} %get-tuple-element.27), channel_id=1, source_target_pairs={{0,4},{4,0},{8,12},{12,8},{16,20},{20,16},{24,28},{28,24},{1,5},{5... | collective-permute-start | bytes 442376 | tf_op jit(solution)/shard_map/ppermute | solution.py:376
  10.5 15.6 %copy-start.7 = (bf16[1,128,1024]{2,1,0:T(8,128)(2,1)S(1)}, bf16[1,128,1024]{2,1,0:T(8,128)(2,1)}, u32[]{:S(2)}) copy-start(bf16[1,128,1024]{2,1,0:T(8,128)(2,1)} %param.11) | copy-start | bytes 786436
  10.5 10.2 %collective-permute-start.3 = (bf16[256,512]{1,0:T(8,128)(2,1)S(1)}, bf16[256,512]{1,0:T(8,128)(2,1)S(1)}, u32[]{:S(2)}, u32[]{:S(2)}) collective-permute-start(bf16[256,512]{1,0:T(8,128)(2,1)S(1)} %get-tuple-element.28.own), channel_id=1, source_target_pairs={{8,0},{16,8},{24,16},{4,12},{12,20},{20,28},{9,1},{17,9},{25,17},{... | collective-permute-start | bytes 786440 | tf_op jit(solution)/shard_map/ppermute | solution.py:376
  12.6 9.2 %collective-permute-start.2 = (bf16[256,512]{1,0:T(8,128)(2,1)S(1)}, bf16[256,512]{1,0:T(8,128)(2,1)S(1)}, u32[]{:S(2)}, u32[]{:S(2)}) collective-permute-start(bf16[256,512]{1,0:T(8,128)(2,1)S(1)} %collective-permute-done.1.par), channel_id=1, source_target_pairs={{0,8},{8,16},{16,24},{12,4},{20,12},{28,20},{1,9},{9,17},{17,25},{... | collective-permute-start | bytes 786440 | tf_op jit(solution)/shard_map/ppermute | solution.py:376
  19.2 9.6 %copy-start = (bf16[1024,1024]{1,0:T(8,128)(2,1)S(1)}, bf16[1024,1024]{1,0:T(8,128)(2,1)}, u32[]{:S(2)}) copy-start(bf16[1024,1024]{1,0:T(8,128)(2,1)} %w.3) | copy-start | bytes 6291460
  19.2 5.6 %collective-permute-start.12 = (bf16[128,1024]{1,0:T(8,128)(2,1)S(1)}, bf16[128,1024]{1,0:T(8,128)(2,1)S(1)}, u32[]{:S(2)}, u32[]{:S(2)}) collective-permute-start(bf16[128,1024]{1,0:T(8,128)(2,1)S(1)} %collective-permute-done.5.cot_par.par), channel_id=1, source_target_pairs={{0,1},{1,0},{2,3},{3,2},{4,5},{5,4},{6,7},{7,6},{8,9},{9,8},{10,11... | collective-permute-start | bytes 786440 | tf_op jit(solution)/shard_map/ppermute | solution.py:377
  20.6 11.9 %copy-start.1 = (bf16[256,512]{1,0:T(8,128)(2,1)}, bf16[256,512]{1,0:T(8,128)(2,1)S(1)}, u32[]{:S(2)}) copy-start(bf16[256,512]{1,0:T(8,128)(2,1)S(1)} %collective-permute-done.3.far_par) | copy-start | bytes 786436
  21.8 10.7 %copy-start.3 = (bf16[256,512]{1,0:T(8,128)(2,1)}, bf16[256,512]{1,0:T(8,128)(2,1)S(1)}, u32[]{:S(2)}) copy-start(bf16[256,512]{1,0:T(8,128)(2,1)S(1)} %collective-permute-done.2.far_own) | copy-start | bytes 786436
  24.0 0.6 %copy-start.21 = (bf16[128,512]{1,0:T(8,128)(2,1)}, bf16[128,512]{1,0:T(8,128)(2,1)S(1)}, u32[]{:S(2)}) copy-start(bf16[128,512]{1,0:T(8,128)(2,1)S(1)} %get-tuple-element.31) | copy-start | bytes 393220
  24.6 7.9 %copy-start.15 = (bf16[128,512]{1,0:T(8,128)(2,1)}, bf16[128,512]{1,0:T(8,128)(2,1)S(1)}, u32[]{:S(2)}) copy-start(bf16[128,512]{1,0:T(8,128)(2,1)S(1)} %get-tuple-element.30.att_own) | copy-start | bytes 393220
  24.6 1.4 %collective-permute-start.10 = (bf16[256,256]{1,0:T(8,128)(2,1)S(1)}, bf16[256,256]{1,0:T(8,128)(2,1)S(1)}, u32[]{:S(2)}, u32[]{:S(2)}) collective-permute-start(bf16[256,256]{1,0:T(8,128)(2,1)S(1)} %get-tuple-element.47), channel_id=1, source_target_pairs={{0,1},{1,0},{2,3},{3,2},{4,5},{5,4},{6,7},{7,6},{8,9},{9,8},{10,11... | collective-permute-start | bytes 393224 | tf_op jit(solution)/shard_map/ppermute | solution.py:377
  27.3 5.3 %copy-start.10 = (f32[128,1024]{1,0:T(8,128)}, f32[128,1024]{1,0:T(8,128)S(1)}, u32[]{:S(2)}) copy-start(f32[128,1024]{1,0:T(8,128)S(1)} %get-tuple-element.45) | copy-start | bytes 1572868
  27.3 18.4 %collective-permute-start.13 = (bf16[128,1024]{1,0:T(8,128)(2,1)}, bf16[128,1024]{1,0:T(8,128)(2,1)}, u32[]{:S(2)}, u32[]{:S(2)}) collective-permute-start(bf16[128,1024]{1,0:T(8,128)(2,1)} %get-tuple-element.46), channel_id=1, source_target_pairs={{0,2},{1,3},{2,0},{3,1},{4,6},{5,7},{6,4},{7,5},{8,10},{9,11},{10,... | collective-permute-start | bytes 786440 | tf_op jit(solution)/shard_map/ppermute | solution.py:413
  32.5 0.9 %copy-start.8 = (bf16[4,384,256]{2,1,0:T(8,128)(2,1)}, bf16[4,384,256]{2,1,0:T(8,128)(2,1)S(1)}, u32[]{:S(2)}) copy-start(bf16[4,384,256]{2,1,0:T(8,128)(2,1)S(1)} %get-tuple-element.34.grads) | copy-start | bytes 2359300
  33.4 0.7 %copy-start.12 = (bf16[256,512]{1,0:T(8,128)(2,1)}, bf16[256,512]{1,0:T(8,128)(2,1)S(1)}, u32[]{:S(2)}) copy-start(bf16[256,512]{1,0:T(8,128)(2,1)S(1)} %get-tuple-element.33.ga) | copy-start | bytes 786436
  34.2 16.4 %collective-permute-start.7 = (bf16[256,512]{1,0:T(8,128)(2,1)}, bf16[256,512]{1,0:T(8,128)(2,1)}, u32[]{:S(2)}, u32[]{:S(2)}) collective-permute-start(bf16[256,512]{1,0:T(8,128)(2,1)} %get-tuple-element.38), channel_id=1, source_target_pairs={{0,8},{4,12},{8,0},{12,4},{16,24},{20,28},{24,16},{28,20},{1,9},{5... | collective-permute-start | bytes 786440 | tf_op jit(solution)/shard_map/ppermute | solution.py:376
  36.7 13.9 %collective-permute-start.8 = (bf16[256,512]{1,0:T(8,128)(2,1)}, bf16[256,512]{1,0:T(8,128)(2,1)}, u32[]{:S(2)}, u32[]{:S(2)}) collective-permute-start(bf16[256,512]{1,0:T(8,128)(2,1)} %get-tuple-element.39), channel_id=1, source_target_pairs={{8,16},{12,20},{16,8},{20,12},{9,17},{13,21},{17,9},{21,13},{10,18... | collective-permute-start | bytes 786440 | tf_op jit(solution)/shard_map/ppermute | solution.py:376
  38.0 17.1 %collective-permute-start.4 = (bf16[128,512]{1,0:T(8,128)(2,1)}, bf16[128,512]{1,0:T(8,128)(2,1)S(1)}, u32[]{:S(2)}, u32[]{:S(2)}) collective-permute-start(bf16[128,512]{1,0:T(8,128)(2,1)} %copy-done.21), channel_id=1, source_target_pairs={{0,4},{4,0},{8,12},{12,8},{16,20},{20,16},{24,28},{28,24},{1,5},{5... | collective-permute-start | bytes 393224 | tf_op jit(solution)/shard_map/ppermute | solution.py:376
  39.6 0.9 %copy-start.2 = (bf16[256,512]{1,0:T(8,128)(2,1)S(1)}, bf16[256,512]{1,0:T(8,128)(2,1)}, u32[]{:S(2)}) copy-start(bf16[256,512]{1,0:T(8,128)(2,1)} %copy-done.1) | copy-start | bytes 786436
  40.6 0.9 %copy-start.4 = (bf16[256,512]{1,0:T(8,128)(2,1)S(1)}, bf16[256,512]{1,0:T(8,128)(2,1)}, u32[]{:S(2)}) copy-start(bf16[256,512]{1,0:T(8,128)(2,1)} %copy-done.3) | copy-start | bytes 786436
  41.5 0.9 %copy-start.6 = (bf16[128,512]{1,0:T(8,128)(2,1)S(1)}, bf16[128,512]{1,0:T(8,128)(2,1)}, u32[]{:S(2)}) copy-start(bf16[128,512]{1,0:T(8,128)(2,1)} %copy-done.5) | copy-start | bytes 393220
  42.4 1.1 %copy-start.9 = (bf16[4,384,256]{2,1,0:T(8,128)(2,1)S(1)}, bf16[4,384,256]{2,1,0:T(8,128)(2,1)}, u32[]{:S(2)}) copy-start(bf16[4,384,256]{2,1,0:T(8,128)(2,1)} %copy-done.8) | copy-start | bytes 2359300
  43.6 0.9 %copy-start.13 = (bf16[256,512]{1,0:T(8,128)(2,1)S(1)}, bf16[256,512]{1,0:T(8,128)(2,1)}, u32[]{:S(2)}) copy-start(bf16[256,512]{1,0:T(8,128)(2,1)} %copy-done.12) | copy-start | bytes 786436
  44.5 1.1 %copy-start.11 = (f32[128,1024]{1,0:T(8,128)S(1)}, f32[128,1024]{1,0:T(8,128)}, u32[]{:S(2)}) copy-start(f32[128,1024]{1,0:T(8,128)} %copy-done.10) | copy-start | bytes 1572868
  45.2 9.9 %copy-start.16 = (bf16[128,512]{1,0:T(8,128)(2,1)S(1)}, bf16[128,512]{1,0:T(8,128)(2,1)}, u32[]{:S(2)}) copy-start(bf16[128,512]{1,0:T(8,128)(2,1)} %copy-done.15) | copy-start | bytes 393220
  45.2 9.9 %copy-start.18 = (s32[2]{0:T(128)S(1)}, s32[2]{0:T(128)}, u32[]{:S(2)}) copy-start(s32[2]{0:T(128)} %copy-done.17) | copy-start | bytes 28
  45.2 11.6 %collective-permute-start.6 = (bf16[128,512]{1,0:T(8,128)(2,1)S(1)}, bf16[128,512]{1,0:T(8,128)(2,1)S(1)}, u32[]{:S(2)}, u32[]{:S(2)}) collective-permute-start(bf16[128,512]{1,0:T(8,128)(2,1)S(1)} %get-tuple-element.36), channel_id=1, source_target_pairs={{0,4},{4,0},{8,12},{12,8},{16,20},{20,16},{24,28},{28,24},{1,5},{5... | collective-permute-start | bytes 393224 | tf_op jit(solution)/shard_map/ppermute | solution.py:376
  46.7 6.8 %collective-permute-start.14 = (bf16[64,1024]{1,0:T(8,128)(2,1)S(1)}, bf16[64,1024]{1,0:T(8,128)(2,1)S(1)}, u32[]{:S(2)}, u32[]{:S(2)}) collective-permute-start(bf16[64,1024]{1,0:T(8,128)(2,1)S(1)} %slice.36), channel_id=1, source_target_pairs={{0,8},{4,12},{8,0},{12,4},{16,24},{20,28},{24,16},{28,20},{1,9},{5... | collective-permute-start | bytes 393224 | tf_op jit(solution)/shard_map/ppermute | solution.py:413
  51.7 6.7 %collective-permute-start.9 = (bf16[256,512]{1,0:T(8,128)(2,1)S(1)}, bf16[256,512]{1,0:T(8,128)(2,1)S(1)}, u32[]{:S(2)}, u32[]{:S(2)}) collective-permute-start(bf16[256,512]{1,0:T(8,128)(2,1)S(1)} %add_convert_fusion), channel_id=1, source_target_pairs={{0,4},{4,0},{8,12},{12,8},{16,20},{20,16},{24,28},{28,24},{1,5},{5... | collective-permute-start | bytes 786440 | tf_op jit(solution)/shard_map/ppermute | solution.py:376
  53.6 6.9 %collective-permute-start.15 = (bf16[32,1024]{1,0:T(8,128)(2,1)S(1)}, bf16[32,1024]{1,0:T(8,128)(2,1)S(1)}, u32[]{:S(2)}, u32[]{:S(2)}) collective-permute-start(bf16[32,1024]{1,0:T(8,128)(2,1)S(1)} %slice.37), channel_id=1, source_target_pairs={{0,16},{4,20},{8,24},{12,28},{16,0},{20,4},{24,8},{28,12},{1,17},{... | collective-permute-start | bytes 196616 | tf_op jit(solution)/shard_map/ppermute | solution.py:413
where the time goes:
time: 61.7 us; the launch traced here: 61.2 us
  starting transfers between devices  23.9 us (39%)
  Pallas kernels  13.9 us (23%)
  local copies, waits for them, and re-layouts  8.83 us (14%)
  waiting for transfers between devices  7.7 us (12%)
  other arithmetic  2.85 us (5%)
  matrix products  2.52 us (4%)
  between operations  1.52 us (2%)
    ppermute x10, starting transfers between devices, on_device(): send = lambda x, pairs: lax.ppermute(x, 'seq', pairs)  16.8 us
    unnamed x44, local copies, waits for them, and re-layouts  8.79 us
    ppermute x3, starting transfers between devices, on_device(): lax.ppermute(out, axis, [(i, i ^ bit) for i in range(count)]).astype(F32)  6.88 us
    ppermute x10, waiting for transfers between devices, on_device(): send = lambda x, pairs: lax.ppermute(x, 'seq', pairs)  4.84 us
    pallas_call x1, Pallas kernels, backward(): call(backward_kernel, (shape_of(*probs.shape),) + (shape_of(2 * tokens, h...  3.75 us
    dot_general x1, matrix products, dot(): lax.dot_general(a, b, (((ca,), (cb,)), ((), ())), preferred_element_type=...  2.52 us
    pallas_call x1, Pallas kernels, forward(): call(functools.partial(forward_kernel, direct, n_dp), (shape_of(pairs, 3...  2.14 us
    pallas_call x1, Pallas kernels, finish_gradients(): call(final_kernel, (shape_of(tokens, 2 * half),) * 3, [SMEM] + [VMEM] * 6...  2.08 us
  transfers between devices with their start and end apart: 16, of which 7 were waited for; matrix products, arithmetic and copies ran while one was open for 8% of the time, Pallas kernels for 18%

commit v1 on v0

--- a/solution.py
+++ b/solution.py
@@ -332,6 +332,18 @@
     )(who, att_own, att_back, w)[0]
 
 
+def returned_kernel(who, d_par, far_a, far_b, total):
+    slot = far_slot(who[0])
+    returned = jnp.where(slot == 0, far_b[...].astype(F32), far_a[...].astype(F32))
+    total[...] = (d_par[...].astype(F32) + returned).astype(BF16)
+
+
+def add_returned(who, d_par, far):
+    return call(
+        returned_kernel, (shape_of(*d_par.shape),), [SMEM] + [VMEM] * 3, "add_returned"
+    )(who, d_par, *far)[0]
+
+
 def final_kernel(who, dq_own, dq_back, own, far_a, far_b, home, dq, dk, dv):
     mine = who[0] & 1
     slot = far_slot(who[0])
@@ -398,8 +410,7 @@
     keep, out = weight_terms(att_t[0], att_core, cot, cot_par, core_own, core_par)
     dq_own, dq_back, d_own, d_par = gradients(inputs, ga, probs, grads)
     dq_back = send(dq_back, swap)
-    returned = jnp.where(far_slot(me) == 0, far[1], far[0])
-    home = send((d_par.astype(F32) + returned.astype(F32)).astype(BF16), swap)
+    home = send(add_returned(who, d_par, far), swap)
 
     hops = []
     bit = 2

time: 61.7 us -> 53.9 us (0.87)
  local copies, waits for them, and re-layouts: 8.83 us -> 1.66 us
  starting transfers between devices: 23.9 us -> 26.1 us
  other arithmetic: 2.85 us -> 0.84 us
  Pallas kernels: 13.9 us -> 12.7 us
    unnamed x44 -> x10, local copies, waits for them, and re-layouts: 8.79 us -> 1.62 us
    ppermute x3, starting transfers between devices: 6.88 us -> 8.79 us  [on_device(): lax.ppermute(out, axis, [(i, i ^ bit) for i in range(count)]).astype(F32)]
    ppermute x10, waiting for transfers between devices: 4.84 us -> 6.23 us  [on_device(): send = lambda x, pairs: lax.ppermute(x, 'seq', pairs)]
    convert_element_type x1 -> x0, other arithmetic: 1.06 us -> none  [on_device(): home = send((d_par.astype(F32) + returned.astype(F32)).astype(BF16), swap)]
    add x3, other arithmetic: 1.72 us -> 0.76 us  [on_device(): keep + lax.ppermute(out, axis, [(i, i ^ bit) for i in range(count)]).asty...]
    ppermute x3, waiting for transfers between devices: 1.54 us -> 0.67 us  [on_device(): lax.ppermute(out, axis, [(i, i ^ bit) for i in range(count)]).astype(F32)]
    pallas_call x1, Pallas kernels: 3.75 us -> 2.97 us  [backward(): call(backward_kernel, (shape_of(*probs.shape),) + (shape_of(2 * tokens, h...]
    pallas_call x0 -> x1, Pallas kernels: none -> 0.64 us  [add_returned(): call(returned_kernel, (shape_of(*d_par.shape),), [SMEM] + [VMEM] * 3, 'ad...]
  transfers between devices with their start and end apart: 16 -> 16, of which waited for: 7 -> 7; matrix products, arithmetic and copies ran while one was open for 8% -> 5% of each run, Pallas kernels for 18% -> 19%
where the time goes in v1:
time: 53.9 us; the launch traced here: 53.5 us
  starting transfers between devices  26.1 us (48%)
  Pallas kernels  12.7 us (24%)
  waiting for transfers between devices  8.22 us (15%)
  matrix products  2.52 us (5%)
  local copies, waits for them, and re-layouts  1.66 us (3%)
  between operations  1.48 us (3%)
  other arithmetic  0.84 us (2%)
    ppermute x10, starting transfers between devices, on_device(): send = lambda x, pairs: lax.ppermute(x, 'seq', pairs)  17.2 us
    ppermute x3, starting transfers between devices, on_device(): lax.ppermute(out, axis, [(i, i ^ bit) for i in range(count)]).astype(F32)  8.79 us
    ppermute x10, waiting for transfers between devices, on_device(): send = lambda x, pairs: lax.ppermute(x, 'seq', pairs)  6.23 us
    pallas_call x1, Pallas kernels, backward(): call(backward_kernel, (shape_of(*probs.shape),) + (shape_of(2 * tokens, h...  2.97 us
    dot_general x1, matrix products, dot(): lax.dot_general(a, b, (((ca,), (cb,)), ((), ())), preferred_element_type=...  2.52 us
    pallas_call x1, Pallas kernels, forward(): call(functools.partial(forward_kernel, direct, n_dp), (shape_of(pairs, 3...  2.14 us
    pallas_call x1, Pallas kernels, finish_output(): call(output_kernel, (shape_of(tokens, w.shape[1]),), [SMEM] + [VMEM] * 3,...  1.71 us
    pallas_call x1, Pallas kernels, pack_kv(): call(pack_kv_kernel, (kv, kv), [SMEM, HBM, HBM], 'pack_keys_values', scra...  1.7 us
  transfers between devices with their start and end apart: 16, of which 7 were waited for; matrix products, arithmetic and copies ran while one was open for 5% of the time, Pallas kernels for 19%

profile of v1, /device:TPU:0, one launch (start us, length us, event | category | flops | bytes accessed | tf_op | source)
XLA Modules:
  0.0 53.5 jit_solution(13287916655798296804)
XLA Ops:
  0.6 0.0 copy-start.4
  0.6 0.1 pad_add_fusion.who
  0.7 1.7 %pack_keys_values.1 = (bf16[256,512]{1,0:T(8,128)(2,1)S(1)}, bf16[256,512]{1,0:T(8,128)(2,1)S(1)}) custom-call(s32[2]{0:T(128)S(1)} %pad_add_fusion.who, bf16[128,1024]{1,0:T(8,128)(2,1)} %bitcast.24, bf16[128,1024]{1,0:T(8,128)(2,1)} %bitcast.25), custom_call_target="tpu_custom_call" | custom-call | tf_op jit(solution)/shard_map/pack_keys_values/pallas_call | solution.py:89
  2.4 3.0 %collective-permute-start.1 = (bf16[256,512]{1,0:T(8,128)(2,1)S(1)}, bf16[256,512]{1,0:T(8,128)(2,1)S(1)}, u32[]{:S(2)}, u32[]{:S(2)}) collective-permute-start(bf16[256,512]{1,0:T(8,128)(2,1)S(1)} %get-tuple-element.29), channel_id=1, source_target_pairs={{0,4},{4,0},{8,12},{12,8},{16,20},{20,16},{24,28},{28,24},{1,5},{5... | collective-permute-start | bytes 786440 | tf_op jit(solution)/shard_map/ppermute | solution.py:388
  5.5 0.0 collective-permute-start.11
  5.5 0.2 collective-permute-start.5
  6.3 0.0 copy-start.2
  6.3 0.9 %copy-done.2 = bf16[1,128,1024]{2,1,0:T(8,128)(2,1)S(1)} copy-done((bf16[1,128,1024]{2,1,0:T(8,128)(2,1)S(1)}, bf16[1,128,1024]{2,1,0:T(8,128)(2,1)}, u32[]{:S(2)}) %copy-start.2) | copy-done | bytes 262168
  7.2 0.0 copy-start.3
  7.2 0.7 %copy-done.3 = s32[1,1,2]{2,1,0:T(1,128)S(1)} copy-done((s32[1,1,2]{2,1,0:T(1,128)S(1)}, s32[1,1,2]{2,1,0:T(1,128)}, u32[]{:S(2)}) %copy-start.3) | copy-done | bytes 32
  7.9 0.6 %pack_queries.1 = (bf16[144,512]{1,0:T(8,128)(2,1)S(1)}, bf16[128,512]{1,0:T(8,128)(2,1)S(1)}) custom-call(s32[2]{0:T(128)S(1)} %pad_add_fusion.who, s32[1,2]{1,0:T(1,128)S(1)} %bitcast.22, s32[1,1]{1,0:T(1,128)S(6)} %copy.12.live, bf16[128,1024]{1,0:T(8,128)(2,1)S(1)} %bitcast.21), custom_call_target="tpu_custom_call" | custom-call | tf_op jit(solution)/shard_map/pack_queries/pallas_call | solution.py:112
  8.5 1.9 %collective-permute-start = (bf16[144,512]{1,0:T(8,128)(2,1)S(1)}, bf16[144,512]{1,0:T(8,128)(2,1)S(1)}, u32[]{:S(2)}, u32[]{:S(2)}) collective-permute-start(bf16[144,512]{1,0:T(8,128)(2,1)S(1)} %get-tuple-element.27), channel_id=1, source_target_pairs={{0,4},{4,0},{8,12},{12,8},{16,20},{20,16},{24,28},{28,24},{1,5},{5... | collective-permute-start | bytes 442376 | tf_op jit(solution)/shard_map/ppermute | solution.py:388
  10.4 0.0 copy-start.1
  10.4 1.4 %collective-permute-start.3 = (bf16[256,512]{1,0:T(8,128)(2,1)S(1)}, bf16[256,512]{1,0:T(8,128)(2,1)S(1)}, u32[]{:S(2)}, u32[]{:S(2)}) collective-permute-start(bf16[256,512]{1,0:T(8,128)(2,1)S(1)} %get-tuple-element.28.own), channel_id=1, source_target_pairs={{8,0},{16,8},{24,16},{4,12},{12,20},{20,28},{9,1},{17,9},{25,17},{... | collective-permute-start | bytes 786440 | tf_op jit(solution)/shard_map/ppermute | solution.py:388
  11.9 0.7 %collective-permute-done.1.par = bf16[256,512]{1,0:T(8,128)(2,1)S(1)} collective-permute-done((bf16[256,512]{1,0:T(8,128)(2,1)S(1)}, bf16[256,512]{1,0:T(8,128)(2,1)S(1)}, u32[]{:S(2)}, u32[]{:S(2)}) %collective-permute-start.1) | collective-permute-done | bytes 262176 | tf_op jit(solution)/shard_map/ppermute | solution.py:388
  12.6 4.0 %collective-permute-start.2 = (bf16[256,512]{1,0:T(8,128)(2,1)S(1)}, bf16[256,512]{1,0:T(8,128)(2,1)S(1)}, u32[]{:S(2)}, u32[]{:S(2)}) collective-permute-start(bf16[256,512]{1,0:T(8,128)(2,1)S(1)} %collective-permute-done.1.par), channel_id=1, source_target_pairs={{0,8},{8,16},{16,24},{12,4},{20,12},{28,20},{1,9},{9,17},{17,25},{... | collective-permute-start | bytes 786440 | tf_op jit(solution)/shard_map/ppermute | solution.py:388
  16.6 2.5 %convolution_convert_fusion.after.ga_full = bf16[128,1024]{1,0:T(8,128)(2,1)S(1)} fusion(bf16[1024,1024]{1,0:T(8,128)(2,1)} %w.3, bf16[1,128,1024]{2,1,0:T(8,128)(2,1)} %param.11), kind=kOutput, calls=%fused_computation | convolution fusion | flops 268566528 | bytes 2621440 | tf_op jit(solution)/shard_map/dot_general | solution.py:23
  19.2 0.0 copy-start
  19.2 0.0 collective-permute-done.5.cot_par.par
  19.2 0.1 collective-permute-start.12
  19.3 1.3 %collective-permute-done.q_par = bf16[144,512]{1,0:T(8,128)(2,1)S(1)} collective-permute-done((bf16[144,512]{1,0:T(8,128)(2,1)S(1)}, bf16[144,512]{1,0:T(8,128)(2,1)S(1)}, u32[]{:S(2)}, u32[]{:S(2)}) %collective-permute-start) | collective-permute-done | bytes 147488 | tf_op jit(solution)/shard_map/ppermute | solution.py:388
  20.5 0.1 collective-permute-done.3.far_par
  20.6 1.2 %collective-permute-done.2.far_own = bf16[256,512]{1,0:T(8,128)(2,1)S(1)} collective-permute-done((bf16[256,512]{1,0:T(8,128)(2,1)S(1)}, bf16[256,512]{1,0:T(8,128)(2,1)S(1)}, u32[]{:S(2)}, u32[]{:S(2)}) %collective-permute-start.2) | collective-permute-done | bytes 262176 | tf_op jit(solution)/shard_map/ppermute | solution.py:388
  21.8 0.0 copy-done.4
  21.8 2.1 %patch_forward.1 = (bf16[4,384,256]{2,1,0:T(8,128)(2,1)S(1)}, bf16[128,512]{1,0:T(8,128)(2,1)S(1)}, bf16[128,512]{1,0:T(8,128)(2,1)S(1)}, bf16[2,256,256]{2,1,0:T(8,128)(2,1)S(1)}) custom-call(s32[2]{0:T(128)S(1)} %pad_add_fusion.who, s32[1,2]{1,0:T(1,128)S(1)} %bitcast.23, s32[1,1]{1,0:T(1,128)S(6)} %copy.12.live, ...), custom_call_target="tpu_custom_call" | custom-call | tf_op jit(solution)/shard_map/patch_forward/pallas_call | solution.py:187
  24.0 0.1 collective-permute-start.10
  24.1 0.0 collective-permute-done.11.core_own
  24.1 0.0 collective-permute-done.12.core_par
  24.1 1.3 %collective-permute-done.10.att_core = bf16[256,256]{1,0:T(8,128)(2,1)S(1)} collective-permute-done((bf16[256,256]{1,0:T(8,128)(2,1)S(1)}, bf16[256,256]{1,0:T(8,128)(2,1)S(1)}, u32[]{:S(2)}, u32[]{:S(2)}) %collective-permute-start.10) | collective-permute-done | bytes 131104 | tf_op jit(solution)/shard_map/ppermute | solution.py:389
  25.4 0.0 copy-done.1
  25.4 0.7 %weight_terms.1 = (f32[128,1024]{1,0:T(8,128)S(1)}, bf16[128,1024]{1,0:T(8,128)(2,1)S(1)}) custom-call(bf16[256,256]{1,0:T(8,128)(2,1)S(1)} %get-tuple-element.48.att_keep, bf16[256,256]{1,0:T(8,128)(2,1)S(1)} %collective-permute-done.10.att_core, bf16[128,1024]{1,0:T(8,128)(2,1)S(1)} %bitcast.20, bf16[128,1024]{1,0:T(8,128)(2,1)S(1)} %collective-permute-done.5.cot_par.par, ...), custom_call_target="tpu_custom_call" | custom-call | tf_op jit(solution)/shard_map/weight_terms/pallas_call | solution.py:307
  26.1 1.6 %collective-permute-start.13 = (bf16[128,1024]{1,0:T(8,128)(2,1)S(1)}, bf16[128,1024]{1,0:T(8,128)(2,1)S(1)}, u32[]{:S(2)}, u32[]{:S(2)}) collective-permute-start(bf16[128,1024]{1,0:T(8,128)(2,1)S(1)} %get-tuple-element.46), channel_id=1, source_target_pairs={{0,2},{1,3},{2,0},{3,1},{4,6},{5,7},{6,4},{7,5},{8,10},{9,11},{10,... | collective-permute-start | bytes 786440 | tf_op jit(solution)/shard_map/ppermute | solution.py:424
  27.7 0.0 copy-done
  27.7 3.0 %patch_backward.1 = (bf16[4,384,256]{2,1,0:T(8,128)(2,1)S(1)}, bf16[256,512]{1,0:T(8,128)(2,1)S(1)}, bf16[256,512]{1,0:T(8,128)(2,1)S(1)}, bf16[256,512]{1,0:T(8,128)(2,1)S(1)}) custom-call(s32[2]{0:T(128)S(1)} %pad_add_fusion.who, bf16[128,512]{1,0:T(8,128)(2,1)S(1)} %get-tuple-element.26.q_own, bf16[144,512]{1,0:T(8,128)(2,1)S(1)} %collective-permute-done.q_par, ...), custom_call_target="tpu_custom_call" | custom-call | tf_op jit(solution)/shard_map/patch_backward/pallas_call | solution.py:251
  30.6 2.6 %collective-permute-start.7 = (bf16[256,512]{1,0:T(8,128)(2,1)S(1)}, bf16[256,512]{1,0:T(8,128)(2,1)S(1)}, u32[]{:S(2)}, u32[]{:S(2)}) collective-permute-start(bf16[256,512]{1,0:T(8,128)(2,1)S(1)} %get-tuple-element.38), channel_id=1, source_target_pairs={{0,8},{4,12},{8,0},{12,4},{16,24},{20,28},{24,16},{28,20},{1,9},{5... | collective-permute-start | bytes 786440 | tf_op jit(solution)/shard_map/ppermute | solution.py:388
  33.2 0.7 %collective-permute-start.8 = (bf16[256,512]{1,0:T(8,128)(2,1)S(1)}, bf16[256,512]{1,0:T(8,128)(2,1)S(1)}, u32[]{:S(2)}, u32[]{:S(2)}) collective-permute-start(bf16[256,512]{1,0:T(8,128)(2,1)S(1)} %get-tuple-element.39), channel_id=1, source_target_pairs={{8,16},{12,20},{16,8},{20,12},{9,17},{13,21},{17,9},{21,13},{10,18... | collective-permute-start | bytes 786440 | tf_op jit(solution)/shard_map/ppermute | solution.py:388
  33.9 0.7 %collective-permute-done.13 = bf16[128,1024]{1,0:T(8,128)(2,1)S(1)} collective-permute-done((bf16[128,1024]{1,0:T(8,128)(2,1)S(1)}, bf16[128,1024]{1,0:T(8,128)(2,1)S(1)}, u32[]{:S(2)}, u32[]{:S(2)}) %collective-permute-start.13) | collective-permute-done | bytes 262176 | tf_op jit(solution)/shard_map/ppermute | solution.py:424
  34.5 0.1 convert_add_fusion
  34.6 3.8 %collective-permute-start.14 = (bf16[64,1024]{1,0:T(8,128)(2,1)S(1)}, bf16[64,1024]{1,0:T(8,128)(2,1)S(1)}, u32[]{:S(2)}, u32[]{:S(2)}) collective-permute-start(bf16[64,1024]{1,0:T(8,128)(2,1)S(1)} %slice.36), channel_id=1, source_target_pairs={{0,8},{4,12},{8,0},{12,4},{16,24},{20,28},{24,16},{28,20},{1,9},{5... | collective-permute-start | bytes 393224 | tf_op jit(solution)/shard_map/ppermute | solution.py:424
  38.4 0.4 collective-permute-start.4
  38.8 0.7 %patch_gradients.1 = (bf16[128,512]{1,0:T(8,128)(2,1)S(1)}, bf16[128,512]{1,0:T(8,128)(2,1)S(1)}, bf16[256,512]{1,0:T(8,128)(2,1)S(1)}, bf16[256,512]{1,0:T(8,128)(2,1)S(1)}) custom-call(bf16[128,512]{1,0:T(8,128)(2,1)S(1)} %get-tuple-element.26.q_own, bf16[144,512]{1,0:T(8,128)(2,1)S(1)} %collective-permute-done.q_par, ...), custom_call_target="tpu_custom_call" | custom-call | tf_op jit(solution)/shard_map/patch_gradients/pallas_call | solution.py:287
  39.5 1.7 %collective-permute-start.6 = (bf16[128,512]{1,0:T(8,128)(2,1)S(1)}, bf16[128,512]{1,0:T(8,128)(2,1)S(1)}, u32[]{:S(2)}, u32[]{:S(2)}) collective-permute-start(bf16[128,512]{1,0:T(8,128)(2,1)S(1)} %get-tuple-element.36), channel_id=1, source_target_pairs={{0,4},{4,0},{8,12},{12,8},{16,20},{20,16},{24,28},{28,24},{1,5},{5... | collective-permute-start | bytes 393224 | tf_op jit(solution)/shard_map/ppermute | solution.py:388
  41.2 0.0 collective-permute-done.7.far_a
  41.2 0.0 collective-permute-done.8.far_b
  41.2 0.6 %add_returned.1 = bf16[256,512]{1,0:T(8,128)(2,1)S(1)} custom-call(s32[2]{0:T(128)S(1)} %pad_add_fusion.who, bf16[256,512]{1,0:T(8,128)(2,1)S(1)} %get-tuple-element.40.d_par, bf16[256,512]{1,0:T(8,128)(2,1)S(1)} %collective-permute-done.7.far_a, bf16[256,512]{1,0:T(8,128)(2,1)S(1)} %collective-permute-done.8.far_b), custom_call_target="tpu_custom_call" | custom-call | tf_op jit(solution)/shard_map/add_returned/pallas_call | solution.py:342
  41.8 1.3 %collective-permute-start.9 = (bf16[256,512]{1,0:T(8,128)(2,1)S(1)}, bf16[256,512]{1,0:T(8,128)(2,1)S(1)}, u32[]{:S(2)}, u32[]{:S(2)}) collective-permute-start(bf16[256,512]{1,0:T(8,128)(2,1)S(1)} %add_returned.1), channel_id=1, source_target_pairs={{0,4},{4,0},{8,12},{12,8},{16,20},{20,16},{24,28},{28,24},{1,5},{5... | collective-permute-start | bytes 786440 | tf_op jit(solution)/shard_map/ppermute | solution.py:388
  43.2 0.0 collective-permute-done.14
  43.2 3.4 %collective-permute-start.15 = (bf16[32,1024]{1,0:T(8,128)(2,1)S(1)}, bf16[32,1024]{1,0:T(8,128)(2,1)S(1)}, u32[]{:S(2)}, u32[]{:S(2)}) collective-permute-start(bf16[32,1024]{1,0:T(8,128)(2,1)S(1)} %slice.37), channel_id=1, source_target_pairs={{0,16},{4,20},{8,24},{12,28},{16,0},{20,4},{24,8},{28,12},{1,17},{... | collective-permute-start | bytes 196616 | tf_op jit(solution)/shard_map/ppermute | solution.py:424
  46.6 0.0 collective-permute-done.4.att_back
  46.6 1.7 %finish_output.1 = bf16[128,1024]{1,0:T(8,128)(2,1)} custom-call(s32[2]{0:T(128)S(1)} %pad_add_fusion.who, bf16[128,512]{1,0:T(8,128)(2,1)S(1)} %get-tuple-element.30.att_own, bf16[128,512]{1,0:T(8,128)(2,1)S(1)} %collective-permute-done.4.att_back, bf16[1024,1024]{1,0:T(8,128)(2,1)S(1)} %copy-done), custom_call_target="tpu_custom_call" | custom-call | tf_op jit(solution)/shard_map/finish_output/pallas_call | solution.py:326
  48.4 0.0 collective-permute-done.6.dq_back
  48.4 2.9 %collective-permute-done.9.home = bf16[256,512]{1,0:T(8,128)(2,1)S(1)} collective-permute-done((bf16[256,512]{1,0:T(8,128)(2,1)S(1)}, bf16[256,512]{1,0:T(8,128)(2,1)S(1)}, u32[]{:S(2)}, u32[]{:S(2)}) %collective-permute-start.9) | collective-permute-done | bytes 262176 | tf_op jit(solution)/shard_map/ppermute | solution.py:388
  51.3 1.6 %finish_gradients.1 = (bf16[128,1024]{1,0:T(8,128)(2,1)}, bf16[128,1024]{1,0:T(8,128)(2,1)}, bf16[128,1024]{1,0:T(8,128)(2,1)}) custom-call(s32[2]{0:T(128)S(1)} %pad_add_fusion.who, bf16[128,512]{1,0:T(8,128)(2,1)S(1)} %get-tuple-element.35.dq_own, bf16[128,512]{1,0:T(8,128)(2,1)S(1)} %collective-permute-done.6.dq_back, ...), custom_call_target="tpu_custom_call" | custom-call | tf_op jit(solution)/shard_map/finish_gradients/pallas_call | solution.py:364
  52.9 0.0 collective-permute-done.15
  52.9 0.7 %slice_add_fusion.1 = f32[32,1024]{1,0:T(8,128)} fusion(f32[64,1024]{1,0:T(8,128)S(1)} %slice_add_fusion, bf16[32,1024]{1,0:T(8,128)(2,1)S(1)} %collective-permute-done.15), kind=kLoop, calls=%fused_computation.5 | loop fusion | flops 65536 | bytes 327680 | tf_op jit(solution)/shard_map/add | solution.py:424
  (4 shorter events, 0.1 us)
Async XLA Ops:
  0.6 21.2 %copy-start.4 = (s32[1,1,2]{2,1,0:T(1,128)S(1)}, s32[1,1,2]{2,1,0:T(1,128)}, u32[]{:S(2)}) copy-start(s32[1,1,2]{2,1,0:T(1,128)} %param.12) | copy-start | bytes 28
  2.4 10.2 %collective-permute-start.1 = (bf16[256,512]{1,0:T(8,128)(2,1)S(1)}, bf16[256,512]{1,0:T(8,128)(2,1)S(1)}, u32[]{:S(2)}, u32[]{:S(2)}) collective-permute-start(bf16[256,512]{1,0:T(8,128)(2,1)S(1)} %get-tuple-element.29), channel_id=1, source_target_pairs={{0,4},{4,0},{8,12},{12,8},{16,20},{20,16},{24,28},{28,24},{1,5},{5... | collective-permute-start | bytes 786440 | tf_op jit(solution)/shard_map/ppermute | solution.py:388
  5.5 18.6 %collective-permute-start.11 = (bf16[128,1024]{1,0:T(8,128)(2,1)}, bf16[128,1024]{1,0:T(8,128)(2,1)S(1)}, u32[]{:S(2)}, u32[]{:S(2)}) collective-permute-start(bf16[128,1024]{1,0:T(8,128)(2,1)} %bitcast.18), channel_id=1, source_target_pairs={{0,1},{1,0},{2,3},{3,2},{4,5},{5,4},{6,7},{7,6},{8,9},{9,8},{10,11... | collective-permute-start | bytes 786440 | tf_op jit(solution)/shard_map/ppermute | solution.py:389
  5.5 13.7 %collective-permute-start.5 = (bf16[128,1024]{1,0:T(8,128)(2,1)}, bf16[128,1024]{1,0:T(8,128)(2,1)S(1)}, u32[]{:S(2)}, u32[]{:S(2)}) collective-permute-start(bf16[128,1024]{1,0:T(8,128)(2,1)} %bitcast.19), channel_id=1, source_target_pairs={{0,4},{4,0},{8,12},{12,8},{16,20},{20,16},{24,28},{28,24},{1,5},{5... | collective-permute-start | bytes 786440 | tf_op jit(solution)/shard_map/ppermute | solution.py:388
  6.3 1.0 %copy-start.2 = (bf16[1,128,1024]{2,1,0:T(8,128)(2,1)S(1)}, bf16[1,128,1024]{2,1,0:T(8,128)(2,1)}, u32[]{:S(2)}) copy-start(bf16[1,128,1024]{2,1,0:T(8,128)(2,1)} %param.7) | copy-start | bytes 786436
  7.2 0.7 %copy-start.3 = (s32[1,1,2]{2,1,0:T(1,128)S(1)}, s32[1,1,2]{2,1,0:T(1,128)}, u32[]{:S(2)}) copy-start(s32[1,1,2]{2,1,0:T(1,128)} %param.12) | copy-start | bytes 28
  8.5 12.0 %collective-permute-start = (bf16[144,512]{1,0:T(8,128)(2,1)S(1)}, bf16[144,512]{1,0:T(8,128)(2,1)S(1)}, u32[]{:S(2)}, u32[]{:S(2)}) collective-permute-start(bf16[144,512]{1,0:T(8,128)(2,1)S(1)} %get-tuple-element.27), channel_id=1, source_target_pairs={{0,4},{4,0},{8,12},{12,8},{16,20},{20,16},{24,28},{28,24},{1,5},{5... | collective-permute-start | bytes 442376 | tf_op jit(solution)/shard_map/ppermute | solution.py:388
  10.4 15.0 %copy-start.1 = (bf16[1,128,1024]{2,1,0:T(8,128)(2,1)S(1)}, bf16[1,128,1024]{2,1,0:T(8,128)(2,1)}, u32[]{:S(2)}) copy-start(bf16[1,128,1024]{2,1,0:T(8,128)(2,1)} %param.11) | copy-start | bytes 786436
  10.4 10.2 %collective-permute-start.3 = (bf16[256,512]{1,0:T(8,128)(2,1)S(1)}, bf16[256,512]{1,0:T(8,128)(2,1)S(1)}, u32[]{:S(2)}, u32[]{:S(2)}) collective-permute-start(bf16[256,512]{1,0:T(8,128)(2,1)S(1)} %get-tuple-element.28.own), channel_id=1, source_target_pairs={{8,0},{16,8},{24,16},{4,12},{12,20},{20,28},{9,1},{17,9},{25,17},{... | collective-permute-start | bytes 786440 | tf_op jit(solution)/shard_map/ppermute | solution.py:388
  12.6 9.2 %collective-permute-start.2 = (bf16[256,512]{1,0:T(8,128)(2,1)S(1)}, bf16[256,512]{1,0:T(8,128)(2,1)S(1)}, u32[]{:S(2)}, u32[]{:S(2)}) collective-permute-start(bf16[256,512]{1,0:T(8,128)(2,1)S(1)} %collective-permute-done.1.par), channel_id=1, source_target_pairs={{0,8},{8,16},{16,24},{12,4},{20,12},{28,20},{1,9},{9,17},{17,25},{... | collective-permute-start | bytes 786440 | tf_op jit(solution)/shard_map/ppermute | solution.py:388
  19.2 8.5 %copy-start = (bf16[1024,1024]{1,0:T(8,128)(2,1)S(1)}, bf16[1024,1024]{1,0:T(8,128)(2,1)}, u32[]{:S(2)}) copy-start(bf16[1024,1024]{1,0:T(8,128)(2,1)} %w.3) | copy-start | bytes 6291460
  19.2 4.9 %collective-permute-start.12 = (bf16[128,1024]{1,0:T(8,128)(2,1)S(1)}, bf16[128,1024]{1,0:T(8,128)(2,1)S(1)}, u32[]{:S(2)}, u32[]{:S(2)}) collective-permute-start(bf16[128,1024]{1,0:T(8,128)(2,1)S(1)} %collective-permute-done.5.cot_par.par), channel_id=1, source_target_pairs={{0,1},{1,0},{2,3},{3,2},{4,5},{5,4},{6,7},{7,6},{8,9},{9,8},{10,11... | collective-permute-start | bytes 786440 | tf_op jit(solution)/shard_map/ppermute | solution.py:389
  24.0 1.4 %collective-permute-start.10 = (bf16[256,256]{1,0:T(8,128)(2,1)S(1)}, bf16[256,256]{1,0:T(8,128)(2,1)S(1)}, u32[]{:S(2)}, u32[]{:S(2)}) collective-permute-start(bf16[256,256]{1,0:T(8,128)(2,1)S(1)} %get-tuple-element.47), channel_id=1, source_target_pairs={{0,1},{1,0},{2,3},{3,2},{4,5},{5,4},{6,7},{7,6},{8,9},{9,8},{10,11... | collective-permute-start | bytes 393224 | tf_op jit(solution)/shard_map/ppermute | solution.py:389
  26.1 8.4 %collective-permute-start.13 = (bf16[128,1024]{1,0:T(8,128)(2,1)S(1)}, bf16[128,1024]{1,0:T(8,128)(2,1)S(1)}, u32[]{:S(2)}, u32[]{:S(2)}) collective-permute-start(bf16[128,1024]{1,0:T(8,128)(2,1)S(1)} %get-tuple-element.46), channel_id=1, source_target_pairs={{0,2},{1,3},{2,0},{3,1},{4,6},{5,7},{6,4},{7,5},{8,10},{9,11},{10,... | collective-permute-start | bytes 786440 | tf_op jit(solution)/shard_map/ppermute | solution.py:424
  30.6 10.5 %collective-permute-start.7 = (bf16[256,512]{1,0:T(8,128)(2,1)S(1)}, bf16[256,512]{1,0:T(8,128)(2,1)S(1)}, u32[]{:S(2)}, u32[]{:S(2)}) collective-permute-start(bf16[256,512]{1,0:T(8,128)(2,1)S(1)} %get-tuple-element.38), channel_id=1, source_target_pairs={{0,8},{4,12},{8,0},{12,4},{16,24},{20,28},{24,16},{28,20},{1,9},{5... | collective-permute-start | bytes 786440 | tf_op jit(solution)/shard_map/ppermute | solution.py:388
  33.2 8.0 %collective-permute-start.8 = (bf16[256,512]{1,0:T(8,128)(2,1)S(1)}, bf16[256,512]{1,0:T(8,128)(2,1)S(1)}, u32[]{:S(2)}, u32[]{:S(2)}) collective-permute-start(bf16[256,512]{1,0:T(8,128)(2,1)S(1)} %get-tuple-element.39), channel_id=1, source_target_pairs={{8,16},{12,20},{16,8},{20,12},{9,17},{13,21},{17,9},{21,13},{10,18... | collective-permute-start | bytes 786440 | tf_op jit(solution)/shard_map/ppermute | solution.py:388
  34.6 8.5 %collective-permute-start.14 = (bf16[64,1024]{1,0:T(8,128)(2,1)S(1)}, bf16[64,1024]{1,0:T(8,128)(2,1)S(1)}, u32[]{:S(2)}, u32[]{:S(2)}) collective-permute-start(bf16[64,1024]{1,0:T(8,128)(2,1)S(1)} %slice.36), channel_id=1, source_target_pairs={{0,8},{4,12},{8,0},{12,4},{16,24},{20,28},{24,16},{28,20},{1,9},{5... | collective-permute-start | bytes 393224 | tf_op jit(solution)/shard_map/ppermute | solution.py:424
  38.4 8.2 %collective-permute-start.4 = (bf16[128,512]{1,0:T(8,128)(2,1)S(1)}, bf16[128,512]{1,0:T(8,128)(2,1)S(1)}, u32[]{:S(2)}, u32[]{:S(2)}) collective-permute-start(bf16[128,512]{1,0:T(8,128)(2,1)S(1)} %get-tuple-element.31), channel_id=1, source_target_pairs={{0,4},{4,0},{8,12},{12,8},{16,20},{20,16},{24,28},{28,24},{1,5},{5... | collective-permute-start | bytes 393224 | tf_op jit(solution)/shard_map/ppermute | solution.py:388
  39.5 8.9 %collective-permute-start.6 = (bf16[128,512]{1,0:T(8,128)(2,1)S(1)}, bf16[128,512]{1,0:T(8,128)(2,1)S(1)}, u32[]{:S(2)}, u32[]{:S(2)}) collective-permute-start(bf16[128,512]{1,0:T(8,128)(2,1)S(1)} %get-tuple-element.36), channel_id=1, source_target_pairs={{0,4},{4,0},{8,12},{12,8},{16,20},{20,16},{24,28},{28,24},{1,5},{5... | collective-permute-start | bytes 393224 | tf_op jit(solution)/shard_map/ppermute | solution.py:388
  41.8 9.5 %collective-permute-start.9 = (bf16[256,512]{1,0:T(8,128)(2,1)S(1)}, bf16[256,512]{1,0:T(8,128)(2,1)S(1)}, u32[]{:S(2)}, u32[]{:S(2)}) collective-permute-start(bf16[256,512]{1,0:T(8,128)(2,1)S(1)} %add_returned.1), channel_id=1, source_target_pairs={{0,4},{4,0},{8,12},{12,8},{16,20},{20,16},{24,28},{28,24},{1,5},{5... | collective-permute-start | bytes 786440 | tf_op jit(solution)/shard_map/ppermute | solution.py:388
  43.2 9.7 %collective-permute-start.15 = (bf16[32,1024]{1,0:T(8,128)(2,1)S(1)}, bf16[32,1024]{1,0:T(8,128)(2,1)S(1)}, u32[]{:S(2)}, u32[]{:S(2)}) collective-permute-start(bf16[32,1024]{1,0:T(8,128)(2,1)S(1)} %slice.37), channel_id=1, source_target_pairs={{0,16},{4,20},{8,24},{12,28},{16,0},{20,4},{24,8},{28,12},{1,17},{... | collective-permute-start | bytes 196616 | tf_op jit(solution)/shard_map/ppermute | solution.py:424
